TPU v7x, 1024 devices: a whole 4x4x32 slice. The times are simulated.
1024 devices in a mesh: orb: 128 (over z, x), aux: 8 (over y, core).
Axes of the slice: x: 4, y: 4, z: 32, core: 2. Of those that a mesh axis runs over, the one named last changes fastest.
Arguments:
- integrals: bfloat16 [128, 8192, 192], P('aux', 'orb'), may hold values from -0.4375 to 0.4375
- coefficients: bfloat16 [8192, 1024], P('orb'), may hold values from -0.09375 to 0.09375
- metric: bfloat16 [128, 128], replicated, may hold values from -0.5 to 0.5
- screening: int32 [8, 128, 3], P('aux', 'orb'), may hold values 0 or 1
Outputs:
- exchange_band: float32 [8192, 192], P('orb')
All inputs are finite; a program needn't handle non-finite values. No bound on the sum of `screening` on one device may be relied on, other than what follows from the above.
Results may differ from a plain program's by a relative error of at most 0.00031.
Values may be sent and summed in bfloat16 or wider, within the bound.
A program may use at most 32 MiB of HBM per device.

v0:
```python
import jax
import jax.numpy as jnp
from jax import lax
from jax.sharding import PartitionSpec as P


def padded(shard, sides, width):
    for axis, dim in sides:
        size, length = (lax.axis_size(axis), shard.shape[dim])
        up = [(i, (i + 1) % size) for i in range(size)]
        down = [(j, i) for i, j in up]
        last = lax.slice_in_dim(shard, length - width, length, axis=dim)
        initial = lax.slice_in_dim(shard, 0, width, axis=dim)
        before = lax.ppermute(last, axis, up)
        after = lax.ppermute(initial, axis, down)
        shard = jnp.concatenate([before, shard, after], axis=dim)
    return shard


def pair_block(left, right):
    return jnp.einsum("pmi,pni->mn", left, right, preferred_element_type=jnp.float32)


def shards(integrals, coefficients, metric, screening):
    block = coefficients.shape[0]
    slab_rows = integrals.shape[0]
    nearby = padded(coefficients, (("orb", 0),), block)
    gate = screening[0, 0]
    weights = jnp.repeat(gate, block).astype(jnp.bfloat16)
    masked = (integrals * weights[None, None, :]).reshape(slab_rows * block, 3 * block)
    half = jnp.dot(masked, nearby, preferred_element_type=jnp.float32)
    half = half.astype(jnp.bfloat16).reshape(slab_rows, block, nearby.shape[1])
    slab = lax.all_to_all(half, "aux", split_axis=2, concat_axis=0, tiled=True)
    flat = slab.reshape(slab.shape[0], slab.shape[1] * slab.shape[2])
    fitted_flat = jnp.dot(metric, flat, preferred_element_type=jnp.float32).astype(jnp.bfloat16)
    fitted = fitted_flat.reshape(metric.shape[0], slab.shape[1], slab.shape[2])
    widened = padded(fitted, (("orb", 1),), block)
    terms = pair_block(fitted, widened)
    total = lax.psum(terms, "aux")
    return total


def solution(mesh):
    in_specs = (P("aux", "orb", None), P("orb", None), P(), P("aux", "orb", None))
    out_specs = P("orb", None)
    return jax.shard_map(shards, mesh=mesh, in_specs=in_specs, out_specs=out_specs, check_vma=False)
```

profile of v0, /device:TPU:1, one launch (start us, length us, event | category | flops | bytes accessed | tf_op | source)
XLA Modules:
  0.0 171.4 jit_solution(12657045749330249377)
XLA Ops:
  0.0 0.0 copy-start
  0.0 4.1 %collective-permute-start = (bf16[64,1024]{1,0:T(8,128)(2,1)}, bf16[64,1024]{1,0:T(8,128)(2,1)S(1)}, u32[]{:S(2)}, u32[]{:S(2)}) collective-permute-start(bf16[64,1024]{1,0:T(8,128)(2,1)} %param.5), channel_id=1, source_target_pairs={{0,8},{8,16},{16,24},{24,32},{32,40},{40,48},{48,56},{56,64},{64,7... | collective-permute-start | bytes 393224 | tf_op jit(solution)/shard_map/ppermute | solution.py:14
  4.1 19.4 %collective-permute-start.1 = (bf16[64,1024]{1,0:T(8,128)(2,1)}, bf16[64,1024]{1,0:T(8,128)(2,1)S(1)}, u32[]{:S(2)}, u32[]{:S(2)}) collective-permute-start(bf16[64,1024]{1,0:T(8,128)(2,1)} %param.5), channel_id=1, source_target_pairs={{8,0},{16,8},{24,16},{32,24},{40,32},{48,40},{56,48},{64,56},{72,6... | collective-permute-start | bytes 393224 | tf_op jit(solution)/shard_map/ppermute | solution.py:15
  23.5 0.7 convert_bitcast_fusion
  24.1 0.1 broadcast_in_dim.4
  24.2 0.1 convert_element_type.25
  24.3 1.1 broadcast_multiply_fusion
  25.4 0.0 collective-permute-done
  25.4 0.5 collective-permute-done.1
  25.9 1.6 convolution_convert_fusion.1
  27.6 4.9 %copy.18 = bf16[16,64,1024]{1,0,2:T(8,128)(2,1)} copy(bf16[16,64,1024]{2,1,0:T(8,128)(2,1)S(1)} %bitcast.27) | data formatting | bytes 4194304 | tf_op jit(solution)/shard_map/reshape | solution.py:32
  32.4 6.4 %reshape.26 = bf16[8,2,65536]{2,1,0:T(2,128)(2,1)S(1)} reshape(bf16[1024,16,64]{2,1,0:T(8,128)(2,1)} %bitcast.25) | data formatting | bytes 4194304
  38.8 32.4 %all_to_all.15 = bf16[8,2,65536]{2,1,0:T(2,128)(2,1)} all-to-all(bf16[8,2,65536]{2,1,0:T(2,128)(2,1)S(1)} %reshape.26), channel_id=1, replica_groups=mesh['orb'=128,'aux'=8] {'aux'}, dimensions={0} | all-to-all | bytes 4194304 | tf_op jit(solution)/shard_map/all_to_all | solution.py:33
  71.2 7.4 %reshape.27 = bf16[1024,16,64]{2,1,0:T(8,128)(2,1)} reshape(bf16[8,2,65536]{2,1,0:T(2,128)(2,1)} %all_to_all.15) | data formatting | bytes 4194304
  78.6 4.9 %copy.20 = bf16[8,16,64,128]{3,2,1,0:T(8,128)(2,1)S(1)} copy(bf16[8,16,64,128]{2,1,3,0:T(8,128)(2,1)} %bitcast.26) | data formatting | bytes 4194304 | tf_op jit(solution)/shard_map/all_to_all | solution.py:33
  83.5 0.0 copy-done
  83.5 2.5 %convolution_convert_fusion = bf16[8192,128]{1,0:T(8,128)(2,1)S(1)} fusion(bf16[128,128]{1,0:T(8,128)(2,1)S(1)} %copy-done, bf16[16,8,64,128]{3,2,1,0:T(8,128)(2,1)S(1)} %bitcast.23), kind=kOutput, calls=%fused_computation | convolution fusion | flops 269484032 | bytes 4227072 | tf_op jit(solution)/shard_map/dot_general | solution.py:35
  86.0 1.4 copy.24
  87.4 7.3 %collective-permute-start.3 = (bf16[128,64,128]{0,1,2:T(8,128)(2,1)S(1)}, bf16[128,64,128]{0,1,2:T(8,128)(2,1)S(1)}, u32[]{:S(2)}, u32[]{:S(2)}) collective-permute-start(bf16[128,64,128]{0,1,2:T(8,128)(2,1)S(1)} %copy.24), channel_id=1, source_target_pairs={{8,0},{16,8},{24,16},{32,24},{40,32},{48,40},{56,48},{64,56},{72,6... | collective-permute-start | bytes 6291464 | tf_op jit(solution)/shard_map/ppermute | solution.py:15
  94.7 1.9 %collective-permute-start.2 = (bf16[128,64,128]{0,1,2:T(8,128)(2,1)S(1)}, bf16[128,64,128]{0,1,2:T(8,128)(2,1)S(1)}, u32[]{:S(2)}, u32[]{:S(2)}) collective-permute-start(bf16[128,64,128]{0,1,2:T(8,128)(2,1)S(1)} %copy.24), channel_id=1, source_target_pairs={{0,8},{8,16},{16,24},{24,32},{32,40},{40,48},{48,56},{56,64},{64,7... | collective-permute-start | bytes 6291464 | tf_op jit(solution)/shard_map/ppermute | solution.py:14
  96.6 41.9 %collective-permute-done.3 = bf16[128,64,128]{0,1,2:T(8,128)(2,1)S(1)} collective-permute-done((bf16[128,64,128]{0,1,2:T(8,128)(2,1)S(1)}, bf16[128,64,128]{0,1,2:T(8,128)(2,1)S(1)}, u32[]{:S(2)}, u32[]{:S(2)}) %collective-permute-start.3) | collective-permute-done | bytes 2097184 | tf_op jit(solution)/shard_map/ppermute | solution.py:15
  138.6 7.2 %collective-permute-done.2 = bf16[128,64,128]{0,1,2:T(8,128)(2,1)S(1)} collective-permute-done((bf16[128,64,128]{0,1,2:T(8,128)(2,1)S(1)}, bf16[128,64,128]{0,1,2:T(8,128)(2,1)S(1)}, u32[]{:S(2)}, u32[]{:S(2)}) %collective-permute-start.2) | collective-permute-done | bytes 2097184 | tf_op jit(solution)/shard_map/ppermute | solution.py:14
  145.7 2.1 %fusion.8 = f32[64,192]{1,0:T(8,128)S(1)} fusion(bf16[128,64,128]{0,1,2:T(8,128)(2,1)S(1)} %copy.24, bf16[128,64,128]{0,1,2:T(8,128)(2,1)S(1)} %collective-permute-done.3, bf16[128,64,128]{0,1,2:T(8,128)(2,1)S(1)} %collective-permute-done.2), kind=kOutput, calls=%fused_computation.10 | convolution fusion | flops 421527552 | bytes 6340608 | tf_op jit(solution)/shard_map/pmi,pni->mn/dot_general | solution.py:21
  147.8 23.6 %psum.7 = f32[64,192]{1,0:T(8,128)} all-reduce(f32[64,192]{1,0:T(8,128)S(1)} %fusion.8), channel_id=1, replica_groups=mesh['orb'=128,'aux'=8] {'aux'}, use_global_device_ids=true, to_apply=%region_0.0 | all-reduce | flops 12288 | bytes 98304 | tf_op jit(solution)/shard_map/psum | solution.py:39
Async XLA Ops:
  0.0 83.5 %copy-start = (bf16[128,128]{1,0:T(8,128)(2,1)S(1)}, bf16[128,128]{1,0:T(8,128)(2,1)}, u32[]{:S(2)}) copy-start(bf16[128,128]{1,0:T(8,128)(2,1)} %param.6) | copy-start | bytes 98308
  0.0 25.4 %collective-permute-start = (bf16[64,1024]{1,0:T(8,128)(2,1)}, bf16[64,1024]{1,0:T(8,128)(2,1)S(1)}, u32[]{:S(2)}, u32[]{:S(2)}) collective-permute-start(bf16[64,1024]{1,0:T(8,128)(2,1)} %param.5), channel_id=1, source_target_pairs={{0,8},{8,16},{16,24},{24,32},{32,40},{40,48},{48,56},{56,64},{64,7... | collective-permute-start | bytes 393224 | tf_op jit(solution)/shard_map/ppermute | solution.py:14
  4.1 21.9 %collective-permute-start.1 = (bf16[64,1024]{1,0:T(8,128)(2,1)}, bf16[64,1024]{1,0:T(8,128)(2,1)S(1)}, u32[]{:S(2)}, u32[]{:S(2)}) collective-permute-start(bf16[64,1024]{1,0:T(8,128)(2,1)} %param.5), channel_id=1, source_target_pairs={{8,0},{16,8},{24,16},{32,24},{40,32},{48,40},{56,48},{64,56},{72,6... | collective-permute-start | bytes 393224 | tf_op jit(solution)/shard_map/ppermute | solution.py:15
  87.4 51.2 %collective-permute-start.3 = (bf16[128,64,128]{0,1,2:T(8,128)(2,1)S(1)}, bf16[128,64,128]{0,1,2:T(8,128)(2,1)S(1)}, u32[]{:S(2)}, u32[]{:S(2)}) collective-permute-start(bf16[128,64,128]{0,1,2:T(8,128)(2,1)S(1)} %copy.24), channel_id=1, source_target_pairs={{8,0},{16,8},{24,16},{32,24},{40,32},{48,40},{56,48},{64,56},{72,6... | collective-permute-start | bytes 6291464 | tf_op jit(solution)/shard_map/ppermute | solution.py:15
  94.7 51.0 %collective-permute-start.2 = (bf16[128,64,128]{0,1,2:T(8,128)(2,1)S(1)}, bf16[128,64,128]{0,1,2:T(8,128)(2,1)S(1)}, u32[]{:S(2)}, u32[]{:S(2)}) collective-permute-start(bf16[128,64,128]{0,1,2:T(8,128)(2,1)S(1)} %copy.24), channel_id=1, source_target_pairs={{0,8},{8,16},{16,24},{24,32},{32,40},{40,48},{48,56},{56,64},{64,7... | collective-permute-start | bytes 6291464 | tf_op jit(solution)/shard_map/ppermute | solution.py:14
where the time goes:
time: 172 us; the launch traced here: 171 us
  blocking collectives  56 us (33%)
  waiting for transfers between devices  49.6 us (29%)
  starting transfers between devices  32.7 us (19%)
  local copies, waits for them, and re-layouts  25.1 us (15%)
  matrix products  6.18 us (4%)
  other arithmetic  1.74 us (1%)
    ppermute x2, waiting for transfers between devices, padded(): after = lax.ppermute(initial, axis, down)  42.5 us
    all_to_all x1, blocking collectives, shards(): slab = lax.all_to_all(half, 'aux', split_axis=2, concat_axis=0, tiled=True)  32.4 us
    ppermute x2, starting transfers between devices, padded(): after = lax.ppermute(initial, axis, down)  26.7 us
    psum x1, blocking collectives, shards(): total = lax.psum(terms, 'aux')  23.6 us
    unnamed x4, local copies, waits for them, and re-layouts  13.8 us
    ppermute x2, waiting for transfers between devices, padded(): before = lax.ppermute(last, axis, up)  7.16 us
    ppermute x2, starting transfers between devices, padded(): before = lax.ppermute(last, axis, up)  5.99 us
    all_to_all x1, local copies, waits for them, and re-layouts, shards(): slab = lax.all_to_all(half, 'aux', split_axis=2, concat_axis=0, tiled=True)  4.93 us
  transfers between devices with their start and end apart: 4, of which 3 were waited for; matrix products, arithmetic and copies ran while one was open for 1% of the time, Pallas kernels for 0%

commit v1 on v0

v1 whole, which is shorter than its diff:
```python
import functools

import jax
import jax.numpy as jnp
from jax import lax
from jax.experimental import pallas as pl
from jax.experimental.pallas import tpu as pltpu
from jax.sharding import PartitionSpec as P

MESH = pl.DeviceIdType.MESH
F32 = jnp.float32
BF16 = jnp.bfloat16
HEAD = (0, 1, 4, 5)
TAIL = (2, 3)
CHUNKS = ((0, 2), (2, 2), (4, 2))


def nn(a, b):
    return lax.dot_general(a, b, (((1,), (0,)), ((), ())), preferred_element_type=F32)


def nt(a, b):
    return lax.dot_general(a, b, (((1,), (1,)), ((), ())), preferred_element_type=F32)


def split(x):
    high = x.astype(BF16)
    return high, (x - high.astype(F32)).astype(BF16)


def iota(shape, dim):
    return lax.broadcasted_iota(jnp.int32, shape, dim)


def fold(x):
    return jnp.concatenate([x[16 * p : 16 * p + 16] for p in range(16)], axis=1)


def kernel(
    n_orb,
    a_ref, c_ref, m_ref, s_ref, o_ref,
    av, cb, ag, mk, psend, precv, ghi, glo, gn, sp_hi, sp_lo, hh, ht, kp, rs, ob,
    load_sem, ag_send, ag_recv, sib_send, sib_recv, c_send, c_recv, g_send, g_recv, r_send, r_recv, b_send, b_recv,
):
    orb = lax.axis_index("orb")
    aux = lax.axis_index("aux")
    y = lax.div(aux, 2)
    core = lax.rem(aux, 2)
    sibling = (orb, 2 * y + 1 - core)
    up = (orb, lax.rem(aux + 2, 8))
    down = (orb, lax.rem(aux + 6, 8))
    after = (lax.rem(orb + 1, n_orb), aux)
    before = (lax.rem(orb + n_orb - 1, n_orb), aux)
    peers = [(orb, lax.rem(aux + j, 8)) for j in range(1, 8)]

    def remote(src, dst, send, recv, target):
        return pltpu.make_async_remote_copy(
            src_ref=src, dst_ref=dst, send_sem=send, recv_sem=recv, device_id=target, device_id_type=MESH
        )

    load_a0 = pltpu.make_async_copy(a_ref.at[:, pl.ds(0, 32), :], av.at[:, pl.ds(0, 32), :], load_sem.at[0])
    load_a1 = pltpu.make_async_copy(a_ref.at[:, pl.ds(32, 32), :], av.at[:, pl.ds(32, 32), :], load_sem.at[1])
    load_c = pltpu.make_async_copy(c_ref, cb.at[2], load_sem.at[2])
    load_a0.start()
    load_c.start()
    load_a1.start()

    barrier = pltpu.get_barrier_semaphore()
    for target in peers + [after, before]:
        pl.semaphore_signal(barrier, inc=1, device_id=target, device_id_type=MESH)

    gate = [s_ref[0, 0, k].astype(F32) for k in range(3)]
    lane = iota((1, 128), 1)
    head_mask = jnp.where(lane < 64, gate[0], gate[1]).astype(BF16)
    rows = pl.ds(pl.multiple_of(256 * y, 256), 256)

    def pack_head(group):
        piece = av[:, 16 * group : 16 * group + 16, 0:128].reshape(256, 128)
        ag[HEAD[group], rows, :] = piece * head_mask

    def pack_tail(which):
        shape = (64, 128)
        low = jnp.where(iota(shape, 0) == iota(shape, 1), gate[2], 0.0).astype(BF16)
        high = jnp.where(iota(shape, 0) + 64 == iota(shape, 1), gate[2], 0.0).astype(BF16)
        first = av[:, 16 * which : 16 * which + 16, 128:192].reshape(256, 64)
        second = av[:, 16 * which + 32 : 16 * which + 48, 128:192].reshape(256, 64)
        ag[TAIL[which], rows, :] = (nn(first, low) + nn(second, high)).astype(BF16)

    load_a0.wait()
    pack_head(0)
    pack_head(1)
    pl.semaphore_wait(barrier, 9)

    def slot(c, index, first, count):
        t, n = CHUNKS[c]
        return ag.at[pl.ds(t, n), pl.ds(pl.multiple_of(256 * index + first, 128), count), :]

    y_up, y_down = lax.rem(y + 1, 4), lax.rem(y + 3, 4)

    def own(c):
        block = slot(c, y, 0, 256)
        return [
            remote(block, block, ag_send.at[c, 0], ag_recv.at[c, 0], up),
            remote(block, block, ag_send.at[c, 1], ag_recv.at[c, 1], down),
        ]

    def relay(c):
        first, second = slot(c, y_down, 0, 128), slot(c, y_up, 128, 128)
        return [
            remote(first, first, ag_send.at[c, 2], ag_recv.at[c, 2], up),
            remote(second, second, ag_send.at[c, 3], ag_recv.at[c, 3], down),
        ]

    owns = [own(c) for c in range(len(CHUNKS))]
    relays = [relay(c) for c in range(len(CHUNKS))]

    def start(copies):
        for copy in copies:
            copy.start()

    start(owns[0])
    load_c.wait()
    coef = [
        remote(cb.at[2], cb.at[1], c_send.at[0], c_recv.at[0], after),
        remote(cb.at[2], cb.at[3], c_send.at[1], c_recv.at[1], before),
    ]
    coef_on = [
        remote(cb.at[1], cb.at[0], c_send.at[2], c_recv.at[2], after),
        remote(cb.at[3], cb.at[4], c_send.at[3], c_recv.at[3], before),
    ]
    start(coef)
    load_a1.wait()
    pack_tail(0)
    pack_tail(1)
    start(owns[1])
    pack_head(2)
    pack_head(3)

    metric_rows = m_ref[pl.ds(pl.multiple_of(32 * y, 32), 32), :]
    column = iota((128, 1024), 1)
    wanted = (2 * (column // 256) + core) * 16 + (column // 16) % 16
    spread = jnp.where(iota((128, 1024), 0) == wanted, 1.0, 0.0).astype(BF16)
    for part in range(4):
        row = iota((128, 32), 0) + 128 * part
        holder = core if part < 2 else 1 - core
        pick = jnp.where(iota((128, 32), 1) == holder * 16 + (row // 16) % 16, 1.0, 0.0).astype(BF16)
        picked = nn(pick, metric_rows).astype(BF16)
        wide = nn(picked, spread)
        same = iota((128, 1024), 0) % 16 == iota((128, 1024), 1) % 16
        mk[128 * part : 128 * part + 128, :] = jnp.where(same, wide, 0.0).astype(BF16)

    def arrive(copies):
        for copy in copies:
            copy.wait_recv()

    arrive(coef)
    start(coef_on)
    arrive(owns[0])
    start(relays[0])
    start(owns[2])

    def gram():
        arrive(coef_on)
        left = cb[1:4].reshape(192, 1024)
        for d in range(3):
            right = jnp.concatenate([cb[d], cb[d + 1], cb[d + 2], cb[d + 2]], axis=0)
            lanes = slice(256 * d, 256 * d + 256)
            zero = jnp.zeros((64, 256), BF16)
            for part, dst in zip(split(nt(left, right)), (sp_hi, sp_lo)):
                dst[0, 0:192, lanes] = part
                dst[0, 192:256, lanes] = zero
                dst[1, 0:128, lanes] = part[0:128]
                dst[1, 128:192, lanes] = zero
                dst[1, 192:256, lanes] = part[128:192]

    def sib(c):
        t, n = CHUNKS[c]
        tiles = pl.ds(t, n)
        return remote(psend.at[tiles], precv.at[tiles], sib_send.at[c], sib_recv.at[c], sibling)

    sibs = [sib(c) for c in range(len(CHUNKS))]

    def near(c):
        t, n = CHUNKS[c]
        tiles = pl.ds(t, n)
        return [
            remote(ghi.at[tiles], gn.at[0, tiles], g_send.at[c, 0], g_recv.at[c, 0], after),
            remote(ghi.at[tiles], gn.at[1, tiles], g_send.at[c, 1], g_recv.at[c, 1], before),
        ]

    nears = [near(c) for c in range(len(CHUNKS))]
    kept = {}

    def mix(c):
        t, n = CHUNKS[c]
        arrive(relays[c])
        panel = jnp.concatenate([ag[i] for i in range(t, t + n)], axis=1)
        other = nn(mk[256:512, :], panel)
        for i in range(n):
            psend[t + i] = other[:, 128 * i : 128 * i + 128]
        sibs[c].start()
        mine = nn(mk[0:256, :], panel)
        kept[c] = mine

    def finish(c):
        t, n = CHUNKS[c]
        sibs[c].wait_recv()
        for i in range(n):
            high, low = split(kept[c][:, 128 * i : 128 * i + 128] + precv[t + i])
            ghi[t + i] = high
            glo[t + i] = low
        start(nears[c])

    low_lanes = iota((256, 128), 1) < 64

    def transform(group):
        par, h, t = group // 2, HEAD[group], TAIL[group % 2]
        high = jnp.concatenate([ghi[h], ghi[t]], axis=1)
        low = jnp.concatenate([glo[h], glo[t]], axis=1)
        for d in range(3):
            lanes = slice(256 * d, 256 * d + 256)
            right = sp_hi[par, :, lanes]
            out = nn(high, right) + nn(low, right) + nn(high, sp_lo[par, :, lanes])
            for at, part in enumerate(split(out)):
                row = slice(64 * at + 16 * group, 64 * at + 16 * group + 16)
                hh[d, row, :] = fold(part[:, 0:128])
                end = part[:, 128:256]
                zero = jnp.zeros_like(end)
                ht[d, row, :] = fold(jnp.where(low_lanes, end, zero))
                row = slice(128 + row.start, 128 + row.stop)
                ht[d, row, :] = fold(jnp.where(low_lanes, zero, end))

    def panel_of(ref, tiles):
        return jnp.concatenate([fold(ref[t]) for t in tiles], axis=0)

    def heads(d, ref, tiles):
        out = nt(hh[d], panel_of(ref, tiles))
        return out[0:64] + out[64:128]

    def tails(d, ref):
        out = nt(ht[d], panel_of(ref, TAIL))
        return out[0:64] + out[64:128], out[128:192] + out[192:256]

    mix(0)
    gram()
    arrive(owns[1])
    start(relays[1])
    finish(0)
    arrive(owns[2])
    start(relays[2])
    mix(1)
    finish(1)
    transform(0)
    transform(1)
    mix(2)
    finish(2)
    transform(2)
    transform(3)

    bands = [None, None, None]
    even, odd = tails(1, ghi)
    first = heads(1, ghi, HEAD[:2]) + even + nt(hh[1, 0:64, :], panel_of(glo, HEAD[:2]))
    second = heads(1, ghi, HEAD[2:]) + odd + nt(hh[1, 0:64, :], panel_of(glo, HEAD[2:]))
    first = first + nt(ht[1, 0:64, :], panel_of(glo, TAIL))
    second = second + nt(ht[1, 128:192, :], panel_of(glo, TAIL))
    bands[1] = (first, second)
    for c in range(2):
        arrive(nears[c])
    partial = {}
    for d, ref in ((0, gn.at[0]), (2, gn.at[1])):
        even, odd = tails(d, ref)
        partial[d] = (heads(d, ref, HEAD[:2]) + even, odd)
    arrive(nears[2])
    for d, ref in ((0, gn.at[0]), (2, gn.at[1])):
        bands[d] = (partial[d][0], partial[d][1] + heads(d, ref, HEAD[2:]))
    kp[...] = jnp.concatenate([part for band in bands for part in band], axis=1)

    scatter = []
    for j, target in enumerate(peers):
        src = kp.at[pl.ds(pl.multiple_of(8 * target[1], 8), 8), :]
        scatter.append(remote(src, rs.at[j], r_send.at[j], r_recv.at[j], target))
    start(scatter)
    mine = pl.ds(pl.multiple_of(8 * aux, 8), 8)
    total = kp[mine, :]
    arrive(scatter)
    for j in range(7):
        total = total + rs[j]
    ob[mine, :] = total
    gather = []
    for j, target in enumerate(peers):
        gather.append(remote(ob.at[mine, :], ob.at[mine, :], b_send.at[j], b_recv.at[j], target))
    start(gather)
    arrive(gather)
    store = pltpu.make_async_copy(ob, o_ref, load_sem.at[3])
    store.start()
    sent = coef + coef_on + sibs + scatter + gather
    for copies in owns + relays + nears:
        sent = sent + copies
    for copy in sent:
        copy.wait_send()
    store.wait()


def shards(n_orb, integrals, coefficients, metric, screening):
    n = len(CHUNKS)
    dma = pltpu.SemaphoreType.DMA
    hbm = pl.BlockSpec(memory_space=pl.ANY)
    return pl.pallas_call(
        functools.partial(kernel, n_orb),
        out_shape=jax.ShapeDtypeStruct((64, 192), F32),
        in_specs=[hbm, hbm, pl.BlockSpec(memory_space=pltpu.VMEM), pl.BlockSpec(memory_space=pltpu.SMEM)],
        out_specs=hbm,
        scratch_shapes=[
            pltpu.VMEM((16, 64, 192), BF16),
            pltpu.VMEM((5, 64, 1024), BF16),
            pltpu.VMEM((6, 1024, 128), BF16),
            pltpu.VMEM((512, 1024), BF16),
            pltpu.VMEM((6, 256, 128), F32),
            pltpu.VMEM((6, 256, 128), F32),
            pltpu.VMEM((6, 256, 128), BF16),
            pltpu.VMEM((6, 256, 128), BF16),
            pltpu.VMEM((2, 6, 256, 128), BF16),
            pltpu.VMEM((2, 256, 768), BF16),
            pltpu.VMEM((2, 256, 768), BF16),
            pltpu.VMEM((3, 128, 2048), BF16),
            pltpu.VMEM((3, 256, 2048), BF16),
            pltpu.VMEM((64, 192), F32),
            pltpu.VMEM((7, 8, 192), F32),
            pltpu.VMEM((64, 192), F32),
            dma((4,)), dma((n, 4)), dma((n, 4)), dma((n,)), dma((n,)), dma((4,)), dma((4,)),
            dma((n, 2)), dma((n, 2)), dma((7,)), dma((7,)), dma((7,)), dma((7,)),
        ],
        compiler_params=pltpu.CompilerParams(
            collective_id=0, has_side_effects=True, vmem_limit_bytes=48 * 1024 * 1024
        ),
    )(integrals, coefficients, metric, screening)


def solution(mesh):
    in_specs = (P("aux", "orb", None), P("orb", None), P(), P("aux", "orb", None))
    body = functools.partial(shards, mesh.shape["orb"])
    return jax.shard_map(body, mesh=mesh, in_specs=in_specs, out_specs=P("orb", None), check_vma=False)
```

time: 172 us -> 62.2 us (0.36)
  Pallas kernels: 0 us -> 57.9 us
  blocking collectives: 56 us -> 0 us
  waiting for transfers between devices: 49.6 us -> 0 us
  starting transfers between devices: 32.7 us -> 0 us
  local copies, waits for them, and re-layouts: 25.1 us -> 3.99 us
  matrix products: 6.18 us -> 0 us
  other arithmetic: 1.74 us -> 0 us
    pallas_call x0 -> x1, Pallas kernels: none -> 57.9 us  [shards(): pl.pallas_call(functools.partial(kernel, n_orb), out_shape=jax.ShapeDtype...]
    ppermute x4 -> x0, waiting for transfers between devices: 49.6 us -> none  [the longest x2 42.5 us: padded(): after = lax.ppermute(initial, axis, down)]
    ppermute x4 -> x0, starting transfers between devices: 32.7 us -> none  [the longest x2 26.7 us: padded(): after = lax.ppermute(initial, axis, down)]
    all_to_all x1 -> x0, blocking collectives: 32.4 us -> none  [shards(): slab = lax.all_to_all(half, 'aux', split_axis=2, concat_axis=0, tiled=True)]
    psum x1 -> x0, blocking collectives: 23.6 us -> none  [shards(): total = lax.psum(terms, 'aux')]
    unnamed x4 -> x9, local copies, waits for them, and re-layouts: 13.8 us -> 3.99 us
    reshape x2 -> x0, local copies, waits for them, and re-layouts: 6.23 us -> none  [the longest x1 4.88 us: shards(): half = half.astype(jnp.bfloat16).reshape(slab_rows, block, nearby.shape[1])]
    dot_general x3 -> x0, matrix products: 6.18 us -> none  [the longest x1 2.49 us: shards(): jnp.dot(metric, flat, preferred_element_type=jnp.float32)]
  transfers between devices with their start and end apart: 4 -> 0, of which waited for: 3 -> 0; matrix products, arithmetic and copies ran while one was open for 1% -> 0% of each run, Pallas kernels for 0% -> 0%
where the time goes in v1:
time: 62.2 us; the launch traced here: 61.9 us
  Pallas kernels  57.9 us (93%)
  local copies, waits for them, and re-layouts  3.99 us (6%)
    pallas_call x1, Pallas kernels, shards(): pl.pallas_call(functools.partial(kernel, n_orb), out_shape=jax.ShapeDtype...  57.9 us
    unnamed x9, local copies, waits for them, and re-layouts  3.99 us

profile of v1, /device:TPU:1, one launch (start us, length us, event | category | flops | bytes accessed | tf_op | source)
XLA Modules:
  0.0 61.9 jit_solution(4201313364258217801)
XLA Ops:
  0.0 0.0 copy-start
  0.0 1.0 %copy-done = bf16[16,64,192]{2,1,0:T(8,128)(2,1)S(1)} copy-done((bf16[16,64,192]{2,1,0:T(8,128)(2,1)S(1)}, bf16[16,64,192]{2,1,0:T(8,128)(2,1)}, u32[]{:S(2)}) %copy-start) | copy-done | bytes 393240
  1.0 0.0 copy-start.1
  1.0 0.9 %copy-done.1 = bf16[64,1024]{1,0:T(8,128)(2,1)S(1)} copy-done((bf16[64,1024]{1,0:T(8,128)(2,1)S(1)}, bf16[64,1024]{1,0:T(8,128)(2,1)}, u32[]{:S(2)}) %copy-start.1) | copy-done | bytes 131096
  1.9 0.0 copy-start.2
  1.9 0.8 %copy-done.2 = bf16[128,128]{1,0:T(8,128)(2,1)S(1)} copy-done((bf16[128,128]{1,0:T(8,128)(2,1)S(1)}, bf16[128,128]{1,0:T(8,128)(2,1)}, u32[]{:S(2)}) %copy-start.2) | copy-done | bytes 32792
  2.7 0.0 copy-start.3
  2.7 0.7 %copy-done.3 = s32[1,1,3]{2,1,0:T(1,128)S(1)} copy-done((s32[1,1,3]{2,1,0:T(1,128)S(1)}, s32[1,1,3]{2,1,0:T(1,128)}, u32[]{:S(2)}) %copy-start.3) | copy-done | bytes 36
  3.4 57.9 %shard_map.46 = f32[64,192]{1,0:T(8,128)S(1)} custom-call(bf16[16,64,192]{2,1,0:T(8,128)(2,1)S(1)} %copy-done, bf16[64,1024]{1,0:T(8,128)(2,1)S(1)} %copy-done.1, bf16[128,128]{1,0:T(8,128)(2,1)S(1)} %copy-done.2, s32[1,1,3]{2,1,0:T(1,128)S(1)} %copy-done.3), custom_call_target="tpu_custom_call" | custom-call | tf_op jit(solution)/shard_map/pallas_call | solution.py:308
  61.3 0.6 %copy.6 = f32[64,192]{1,0:T(8,128)} copy(f32[64,192]{1,0:T(8,128)S(1)} %shard_map.46) | data formatting | bytes 98304
Async XLA Ops:
  0.0 1.0 %copy-start = (bf16[16,64,192]{2,1,0:T(8,128)(2,1)S(1)}, bf16[16,64,192]{2,1,0:T(8,128)(2,1)}, u32[]{:S(2)}) copy-start(bf16[16,64,192]{2,1,0:T(8,128)(2,1)} %a_ref.1) | copy-start | bytes 1179652
  1.0 0.9 %copy-start.1 = (bf16[64,1024]{1,0:T(8,128)(2,1)S(1)}, bf16[64,1024]{1,0:T(8,128)(2,1)}, u32[]{:S(2)}) copy-start(bf16[64,1024]{1,0:T(8,128)(2,1)} %c_ref.1) | copy-start | bytes 393220
  1.9 0.8 %copy-start.2 = (bf16[128,128]{1,0:T(8,128)(2,1)S(1)}, bf16[128,128]{1,0:T(8,128)(2,1)}, u32[]{:S(2)}) copy-start(bf16[128,128]{1,0:T(8,128)(2,1)} %m_ref.1) | copy-start | bytes 98308
  2.7 0.7 %copy-start.3 = (s32[1,1,3]{2,1,0:T(1,128)S(1)}, s32[1,1,3]{2,1,0:T(1,128)}, u32[]{:S(2)}) copy-start(s32[1,1,3]{2,1,0:T(1,128)} %s_ref.1) | copy-start | bytes 40

commit v2 on v1

--- a/solution.py
+++ b/solution.py
@@ -10,9 +10,9 @@
 MESH = pl.DeviceIdType.MESH
 F32 = jnp.float32
 BF16 = jnp.bfloat16
-HEAD = (0, 1, 4, 5)
-TAIL = (2, 3)
-CHUNKS = ((0, 2), (2, 2), (4, 2))
+HEAD = (0, 4, 2, 5)
+TAIL = (1, 3)
+CHUNKS = tuple((t, 1) for t in range(6))
 
 
 def nn(a, b):
@@ -38,8 +38,8 @@
 
 def kernel(
     n_orb,
-    a_ref, c_ref, m_ref, s_ref, o_ref,
-    av, cb, ag, mk, psend, precv, ghi, glo, gn, sp_hi, sp_lo, hh, ht, kp, rs, ob,
+    a_ref, c_ref, metric_ref, screen_ref, o_ref,
+    av, m_ref, s_ref, cb, ag, mk, psend, precv, ghi, glo, gn, sp_hi, sp_lo, hh, ht, kp, kr, quad, ob,
     load_sem, ag_send, ag_recv, sib_send, sib_recv, c_send, c_recv, g_send, g_recv, r_send, r_recv, b_send, b_recv,
 ):
     orb = lax.axis_index("orb")
@@ -51,7 +51,7 @@
     down = (orb, lax.rem(aux + 6, 8))
     after = (lax.rem(orb + 1, n_orb), aux)
     before = (lax.rem(orb + n_orb - 1, n_orb), aux)
-    peers = [(orb, lax.rem(aux + j, 8)) for j in range(1, 8)]
+    across = (orb, lax.rem(aux + 4, 8))
 
     def remote(src, dst, send, recv, target):
         return pltpu.make_async_remote_copy(
@@ -61,14 +61,19 @@
     load_a0 = pltpu.make_async_copy(a_ref.at[:, pl.ds(0, 32), :], av.at[:, pl.ds(0, 32), :], load_sem.at[0])
     load_a1 = pltpu.make_async_copy(a_ref.at[:, pl.ds(32, 32), :], av.at[:, pl.ds(32, 32), :], load_sem.at[1])
     load_c = pltpu.make_async_copy(c_ref, cb.at[2], load_sem.at[2])
+    load_s = pltpu.make_async_copy(screen_ref, s_ref, load_sem.at[3])
+    load_m = pltpu.make_async_copy(metric_ref, m_ref, load_sem.at[4])
+    load_s.start()
     load_a0.start()
     load_c.start()
     load_a1.start()
+    load_m.start()
 
     barrier = pltpu.get_barrier_semaphore()
-    for target in peers + [after, before]:
+    for target in (sibling, up, down, across, after, before):
         pl.semaphore_signal(barrier, inc=1, device_id=target, device_id_type=MESH)
 
+    load_s.wait()
     gate = [s_ref[0, 0, k].astype(F32) for k in range(3)]
     lane = iota((1, 128), 1)
     head_mask = jnp.where(lane < 64, gate[0], gate[1]).astype(BF16)
@@ -87,9 +92,9 @@
         ag[TAIL[which], rows, :] = (nn(first, low) + nn(second, high)).astype(BF16)
 
     load_a0.wait()
+    load_a1.wait()
     pack_head(0)
-    pack_head(1)
-    pl.semaphore_wait(barrier, 9)
+    pl.semaphore_wait(barrier, 6)
 
     def slot(c, index, first, count):
         t, n = CHUNKS[c]
@@ -118,8 +123,10 @@
         for copy in copies:
             copy.start()
 
-    start(owns[0])
-    load_c.wait()
+    def arrive(copies):
+        for copy in copies:
+            copy.wait_recv()
+
     coef = [
         remote(cb.at[2], cb.at[1], c_send.at[0], c_recv.at[0], after),
         remote(cb.at[2], cb.at[3], c_send.at[1], c_recv.at[1], before),
@@ -128,13 +135,17 @@
         remote(cb.at[1], cb.at[0], c_send.at[2], c_recv.at[2], after),
         remote(cb.at[3], cb.at[4], c_send.at[3], c_recv.at[3], before),
     ]
+    start(owns[0])
+    pack_tail(0)
+    start(owns[1])
+    load_c.wait()
     start(coef)
-    load_a1.wait()
-    pack_tail(0)
+    pack_head(2)
+    start(owns[2])
     pack_tail(1)
-    start(owns[1])
-    pack_head(2)
+    pack_head(1)
     pack_head(3)
+    load_m.wait()
 
     metric_rows = m_ref[pl.ds(pl.multiple_of(32 * y, 32), 32), :]
     column = iota((128, 1024), 1)
@@ -148,16 +159,6 @@
         wide = nn(picked, spread)
         same = iota((128, 1024), 0) % 16 == iota((128, 1024), 1) % 16
         mk[128 * part : 128 * part + 128, :] = jnp.where(same, wide, 0.0).astype(BF16)
-
-    def arrive(copies):
-        for copy in copies:
-            copy.wait_recv()
-
-    arrive(coef)
-    start(coef_on)
-    arrive(owns[0])
-    start(relays[0])
-    start(owns[2])
 
     def gram():
         arrive(coef_on)
@@ -241,20 +242,39 @@
         out = nt(ht[d], panel_of(ref, TAIL))
         return out[0:64] + out[64:128], out[128:192] + out[192:256]
 
-    mix(0)
-    gram()
+    arrive(owns[0])
+    start(relays[0])
+    start(owns[3])
     arrive(owns[1])
     start(relays[1])
-    finish(0)
+    start(owns[4])
+    arrive(coef)
+    start(coef_on)
     arrive(owns[2])
     start(relays[2])
+    start(owns[5])
+    mix(0)
+    arrive(owns[3])
+    start(relays[3])
+    finish(0)
     mix(1)
+    arrive(owns[4])
+    start(relays[4])
+    mix(2)
     finish(1)
+    arrive(owns[5])
+    start(relays[5])
+    finish(2)
+    gram()
+    mix(3)
+    mix(4)
+    finish(3)
+    mix(5)
+    finish(4)
     transform(0)
+    finish(5)
+    transform(2)
     transform(1)
-    mix(2)
-    finish(2)
-    transform(2)
     transform(3)
 
     bands = [None, None, None]
@@ -264,54 +284,59 @@
     first = first + nt(ht[1, 0:64, :], panel_of(glo, TAIL))
     second = second + nt(ht[1, 128:192, :], panel_of(glo, TAIL))
     bands[1] = (first, second)
-    for c in range(2):
+    for c in range(5):
         arrive(nears[c])
     partial = {}
     for d, ref in ((0, gn.at[0]), (2, gn.at[1])):
         even, odd = tails(d, ref)
-        partial[d] = (heads(d, ref, HEAD[:2]) + even, odd)
-    arrive(nears[2])
+        partial[d] = (heads(d, ref, HEAD[:2]) + even, heads(d, ref, HEAD[2:3]), odd)
+    arrive(nears[5])
     for d, ref in ((0, gn.at[0]), (2, gn.at[1])):
-        bands[d] = (partial[d][0], partial[d][1] + heads(d, ref, HEAD[2:]))
-    kp[...] = jnp.concatenate([part for band in bands for part in band], axis=1)
-
-    scatter = []
-    for j, target in enumerate(peers):
-        src = kp.at[pl.ds(pl.multiple_of(8 * target[1], 8), 8), :]
-        scatter.append(remote(src, rs.at[j], r_send.at[j], r_recv.at[j], target))
-    start(scatter)
-    mine = pl.ds(pl.multiple_of(8 * aux, 8), 8)
-    total = kp[mine, :]
-    arrive(scatter)
-    for j in range(7):
-        total = total + rs[j]
-    ob[mine, :] = total
+        done, third, odd = partial[d]
+        bands[d] = (done, jnp.concatenate([third, heads(d, ref, HEAD[3:])], axis=1) + odd)
+    kp[0:64, :] = jnp.concatenate(bands[0] + bands[1], axis=1)
+    last = jnp.concatenate(bands[2], axis=1)
+    kp[64:96, :] = jnp.concatenate([last[0:32], last[32:64]], axis=1)
+
+    mine = pl.ds(pl.multiple_of(48 * core, 16), 48)
+    other = pl.ds(pl.multiple_of(48 * (1 - core), 16), 48)
+    pair = remote(kp.at[other, :], kr, r_send.at[0], r_recv.at[0], sibling)
+    pair.start()
+    pair.wait_recv()
+    quad[y] = kp[mine, :] + kr[...]
     gather = []
-    for j, target in enumerate(peers):
-        gather.append(remote(ob.at[mine, :], ob.at[mine, :], b_send.at[j], b_recv.at[j], target))
+    for j, target in enumerate((up, down, across)):
+        gather.append(remote(quad.at[y], quad.at[y], b_send.at[j], b_recv.at[j], target))
     start(gather)
     arrive(gather)
-    store = pltpu.make_async_copy(ob, o_ref, load_sem.at[3])
-    store.start()
-    sent = coef + coef_on + sibs + scatter + gather
+    ob[mine, :] = (quad[0] + quad[1]) + (quad[2] + quad[3])
+    share = remote(ob.at[mine, :], ob.at[mine, :], r_send.at[1], r_recv.at[1], sibling)
+    share.start()
+    share.wait_recv()
+    pair.wait_send()
+    end = ob[64:96, :]
+    right = jnp.concatenate([end[:, 0:64], end[:, 64:128]], axis=0)
+    o_ref[...] = jnp.concatenate([ob[0:64, :], right], axis=1)
+    sent = coef + coef_on + sibs + gather + [share]
     for copies in owns + relays + nears:
         sent = sent + copies
     for copy in sent:
         copy.wait_send()
-    store.wait()
 
 
 def shards(n_orb, integrals, coefficients, metric, screening):
     n = len(CHUNKS)
     dma = pltpu.SemaphoreType.DMA
-    hbm = pl.BlockSpec(memory_space=pl.ANY)
+    hbm = pl.BlockSpec(memory_space=pltpu.HBM)
     return pl.pallas_call(
         functools.partial(kernel, n_orb),
         out_shape=jax.ShapeDtypeStruct((64, 192), F32),
-        in_specs=[hbm, hbm, pl.BlockSpec(memory_space=pltpu.VMEM), pl.BlockSpec(memory_space=pltpu.SMEM)],
-        out_specs=hbm,
+        in_specs=[hbm, hbm, hbm, hbm],
+        out_specs=pl.BlockSpec(memory_space=pltpu.VMEM),
         scratch_shapes=[
             pltpu.VMEM((16, 64, 192), BF16),
+            pltpu.VMEM((128, 128), BF16),
+            pltpu.SMEM((1, 1, 3), jnp.int32),
             pltpu.VMEM((5, 64, 1024), BF16),
             pltpu.VMEM((6, 1024, 128), BF16),
             pltpu.VMEM((512, 1024), BF16),
@@ -324,14 +349,15 @@
             pltpu.VMEM((2, 256, 768), BF16),
             pltpu.VMEM((3, 128, 2048), BF16),
             pltpu.VMEM((3, 256, 2048), BF16),
-            pltpu.VMEM((64, 192), F32),
-            pltpu.VMEM((7, 8, 192), F32),
-            pltpu.VMEM((64, 192), F32),
-            dma((4,)), dma((n, 4)), dma((n, 4)), dma((n,)), dma((n,)), dma((4,)), dma((4,)),
-            dma((n, 2)), dma((n, 2)), dma((7,)), dma((7,)), dma((7,)), dma((7,)),
+            pltpu.VMEM((96, 128), F32),
+            pltpu.VMEM((48, 128), F32),
+            pltpu.VMEM((4, 48, 128), F32),
+            pltpu.VMEM((96, 128), F32),
+            dma((5,)), dma((n, 4)), dma((n, 4)), dma((n,)), dma((n,)), dma((4,)), dma((4,)),
+            dma((n, 2)), dma((n, 2)), dma((2,)), dma((2,)), dma((3,)), dma((3,)),
         ],
         compiler_params=pltpu.CompilerParams(
-            collective_id=0, has_side_effects=True, vmem_limit_bytes=48 * 1024 * 1024
+            collective_id=0, has_side_effects=True, vmem_limit_bytes=62 * 1024 * 1024
         ),
     )(integrals, coefficients, metric, screening)
 

time: 62.2 us -> 55.6 us (0.89)
  Pallas kernels: 57.9 us -> 53.9 us
  local copies, waits for them, and re-layouts: 3.99 us -> 1.47 us
    pallas_call x1, Pallas kernels: 57.9 us -> 53.9 us  [shards(): pl.pallas_call(functools.partial(kernel, n_orb), out_shape=jax.ShapeDtype...]
    unnamed x9 -> x1, local copies, waits for them, and re-layouts: 3.99 us -> 1.47 us
where the time goes in v2:
time: 55.6 us; the launch traced here: 55.4 us
  Pallas kernels  53.9 us (97%)
  local copies, waits for them, and re-layouts  1.47 us (3%)
    pallas_call x1, Pallas kernels, shards(): pl.pallas_call(functools.partial(kernel, n_orb), out_shape=jax.ShapeDtype...  53.9 us
    unnamed x1, local copies, waits for them, and re-layouts  1.47 us

profile of v2, /device:TPU:1, one launch (start us, length us, event | category | flops | bytes accessed | tf_op | source)
XLA Modules:
  0.0 55.4 jit_solution(16323404318627107439)
XLA Ops:
  0.0 53.9 %shard_map.46 = f32[64,192]{1,0:T(8,128)} custom-call(bf16[16,64,192]{2,1,0:T(8,128)(2,1)} %a_ref.1, bf16[64,1024]{1,0:T(8,128)(2,1)} %c_ref.1, bf16[128,128]{1,0:T(8,128)(2,1)} %metric_ref.1, s32[1,1,3]{2,1,0:T(1,128)} %screen_ref.1), custom_call_target="tpu_custom_call" | custom-call | tf_op jit(solution)/shard_map/pallas_call | solution.py:331
  54.0 1.5 %copy.6 = f32[64,192]{1,0:T(8,128)} copy(f32[64,192]{1,0:T(8,128)} %shard_map.46) | data formatting | bytes 98304

commit v3 on v2

--- a/solution.py
+++ b/solution.py
@@ -39,7 +39,7 @@
 def kernel(
     n_orb,
     a_ref, c_ref, metric_ref, screen_ref, o_ref,
-    av, m_ref, s_ref, cb, ag, mk, psend, precv, ghi, glo, gn, sp_hi, sp_lo, hh, ht, kp, kr, quad, ob,
+    av, m_ref, s_ref, cb, ag, mk, psend, precv, ghi, glo, gn, sp_hi, sp_lo, hh, ht, kp, kr, quad, ob, late,
     load_sem, ag_send, ag_recv, sib_send, sib_recv, c_send, c_recv, g_send, g_recv, r_send, r_recv, b_send, b_recv,
 ):
     orb = lax.axis_index("orb")
@@ -52,6 +52,7 @@
     after = (lax.rem(orb + 1, n_orb), aux)
     before = (lax.rem(orb + n_orb - 1, n_orb), aux)
     across = (orb, lax.rem(aux + 4, 8))
+    peers = [(orb, lax.rem(aux + j, 8)) for j in range(1, 8)]
 
     def remote(src, dst, send, recv, target):
         return pltpu.make_async_remote_copy(
@@ -70,18 +71,17 @@
     load_m.start()
 
     barrier = pltpu.get_barrier_semaphore()
-    for target in (sibling, up, down, across, after, before):
+    for target in peers + [after, before]:
         pl.semaphore_signal(barrier, inc=1, device_id=target, device_id_type=MESH)
 
     load_s.wait()
     gate = [s_ref[0, 0, k].astype(F32) for k in range(3)]
     lane = iota((1, 128), 1)
     head_mask = jnp.where(lane < 64, gate[0], gate[1]).astype(BF16)
-    rows = pl.ds(pl.multiple_of(256 * y, 256), 256)
 
     def pack_head(group):
         piece = av[:, 16 * group : 16 * group + 16, 0:128].reshape(256, 128)
-        ag[HEAD[group], rows, :] = piece * head_mask
+        ag[HEAD[group], 0:256, :] = piece * head_mask
 
     def pack_tail(which):
         shape = (64, 128)
@@ -89,31 +89,28 @@
         high = jnp.where(iota(shape, 0) + 64 == iota(shape, 1), gate[2], 0.0).astype(BF16)
         first = av[:, 16 * which : 16 * which + 16, 128:192].reshape(256, 64)
         second = av[:, 16 * which + 32 : 16 * which + 48, 128:192].reshape(256, 64)
-        ag[TAIL[which], rows, :] = (nn(first, low) + nn(second, high)).astype(BF16)
+        ag[TAIL[which], 0:256, :] = (nn(first, low) + nn(second, high)).astype(BF16)
 
     load_a0.wait()
     load_a1.wait()
     pack_head(0)
-    pl.semaphore_wait(barrier, 6)
-
-    def slot(c, index, first, count):
-        t, n = CHUNKS[c]
-        return ag.at[pl.ds(t, n), pl.ds(pl.multiple_of(256 * index + first, 128), count), :]
-
-    y_up, y_down = lax.rem(y + 1, 4), lax.rem(y + 3, 4)
+    pl.semaphore_wait(barrier, 9)
+
+    def slot(c, place, first, count):
+        t, n = CHUNKS[c]
+        return ag.at[pl.ds(t, n), pl.ds(256 * place + first, count), :]
 
     def own(c):
-        block = slot(c, y, 0, 256)
+        block = slot(c, 0, 0, 256)
         return [
-            remote(block, block, ag_send.at[c, 0], ag_recv.at[c, 0], up),
-            remote(block, block, ag_send.at[c, 1], ag_recv.at[c, 1], down),
+            remote(block, slot(c, 2, 0, 256), ag_send.at[c, 0], ag_recv.at[c, 0], up),
+            remote(block, slot(c, 1, 0, 256), ag_send.at[c, 1], ag_recv.at[c, 1], down),
         ]
 
     def relay(c):
-        first, second = slot(c, y_down, 0, 128), slot(c, y_up, 128, 128)
         return [
-            remote(first, first, ag_send.at[c, 2], ag_recv.at[c, 2], up),
-            remote(second, second, ag_send.at[c, 3], ag_recv.at[c, 3], down),
+            remote(slot(c, 2, 0, 128), slot(c, 3, 0, 128), ag_send.at[c, 2], ag_recv.at[c, 2], up),
+            remote(slot(c, 1, 128, 128), slot(c, 3, 128, 128), ag_send.at[c, 3], ag_recv.at[c, 3], down),
         ]
 
     owns = [own(c) for c in range(len(CHUNKS))]
@@ -149,7 +146,9 @@
 
     metric_rows = m_ref[pl.ds(pl.multiple_of(32 * y, 32), 32), :]
     column = iota((128, 1024), 1)
-    wanted = (2 * (column // 256) + core) * 16 + (column // 16) % 16
+    place = column // 256
+    chip = (y + jnp.where(place < 2, place, 5 - place)) % 4
+    wanted = (2 * chip + core) * 16 + (column // 16) % 16
     spread = jnp.where(iota((128, 1024), 0) == wanted, 1.0, 0.0).astype(BF16)
     for part in range(4):
         row = iota((128, 32), 0) + 128 * part
@@ -192,16 +191,22 @@
     nears = [near(c) for c in range(len(CHUNKS))]
     kept = {}
 
+    early = {}
+
+    def premix(c):
+        t, n = CHUNKS[c]
+        panel = jnp.concatenate([ag[i, 0:768, :] for i in range(t, t + n)], axis=1)
+        early[c] = nn(mk[:, 0:768], panel)
+
     def mix(c):
         t, n = CHUNKS[c]
         arrive(relays[c])
-        panel = jnp.concatenate([ag[i] for i in range(t, t + n)], axis=1)
-        other = nn(mk[256:512, :], panel)
+        panel = jnp.concatenate([ag[i, 768:1024, :] for i in range(t, t + n)], axis=1)
+        other = early[c][256:512] + nn(mk[256:512, 768:1024], panel)
         for i in range(n):
             psend[t + i] = other[:, 128 * i : 128 * i + 128]
         sibs[c].start()
-        mine = nn(mk[0:256, :], panel)
-        kept[c] = mine
+        kept[c] = early[c][0:256] + nn(mk[0:256, 768:1024], panel)
 
     def finish(c):
         t, n = CHUNKS[c]
@@ -240,63 +245,66 @@
 
     def tails(d, ref):
         out = nt(ht[d], panel_of(ref, TAIL))
-        return out[0:64] + out[64:128], out[128:192] + out[192:256]
+        return jnp.concatenate([out[0:64] + out[64:128], out[128:192] + out[192:256]], axis=1)
+
+    def diagonal():
+        out = nt(hh[1], jnp.concatenate([panel_of(ghi, HEAD), panel_of(glo, HEAD)], axis=0))
+        head = out[0:64, 0:64] + out[64:128, 0:64] + out[0:64, 64:128]
+        out = nt(ht[1], jnp.concatenate([panel_of(ghi, TAIL), panel_of(glo, TAIL)], axis=0))
+        even = out[0:64, 0:32] + out[64:128, 0:32] + out[0:64, 32:64]
+        odd = out[128:192, 0:32] + out[192:256, 0:32] + out[128:192, 32:64]
+        return head + jnp.concatenate([even, odd], axis=1)
 
     arrive(owns[0])
     start(relays[0])
     start(owns[3])
+    premix(0)
     arrive(owns[1])
     start(relays[1])
     start(owns[4])
+    premix(1)
     arrive(coef)
     start(coef_on)
     arrive(owns[2])
     start(relays[2])
     start(owns[5])
+    premix(2)
     mix(0)
     arrive(owns[3])
     start(relays[3])
+    premix(3)
+    mix(1)
     finish(0)
-    mix(1)
     arrive(owns[4])
     start(relays[4])
+    premix(4)
     mix(2)
     finish(1)
+    gram()
     arrive(owns[5])
     start(relays[5])
     finish(2)
-    gram()
+    premix(5)
     mix(3)
+    transform(0)
     mix(4)
     finish(3)
     mix(5)
     finish(4)
-    transform(0)
+    transform(2)
     finish(5)
-    transform(2)
     transform(1)
     transform(3)
 
-    bands = [None, None, None]
-    even, odd = tails(1, ghi)
-    first = heads(1, ghi, HEAD[:2]) + even + nt(hh[1, 0:64, :], panel_of(glo, HEAD[:2]))
-    second = heads(1, ghi, HEAD[2:]) + odd + nt(hh[1, 0:64, :], panel_of(glo, HEAD[2:]))
-    first = first + nt(ht[1, 0:64, :], panel_of(glo, TAIL))
-    second = second + nt(ht[1, 128:192, :], panel_of(glo, TAIL))
-    bands[1] = (first, second)
-    for c in range(5):
+    bands = [None, diagonal(), None]
+    for c in range(4):
         arrive(nears[c])
-    partial = {}
+    blank = jnp.zeros((64, 16), F32)
     for d, ref in ((0, gn.at[0]), (2, gn.at[1])):
-        even, odd = tails(d, ref)
-        partial[d] = (heads(d, ref, HEAD[:2]) + even, heads(d, ref, HEAD[2:3]), odd)
-    arrive(nears[5])
-    for d, ref in ((0, gn.at[0]), (2, gn.at[1])):
-        done, third, odd = partial[d]
-        bands[d] = (done, jnp.concatenate([third, heads(d, ref, HEAD[3:])], axis=1) + odd)
-    kp[0:64, :] = jnp.concatenate(bands[0] + bands[1], axis=1)
-    last = jnp.concatenate(bands[2], axis=1)
-    kp[64:96, :] = jnp.concatenate([last[0:32], last[32:64]], axis=1)
+        out = heads(d, ref, HEAD[0::2])
+        bands[d] = jnp.concatenate([out[:, 0:16], blank, out[:, 16:32], blank], axis=1) + tails(d, ref)
+    kp[0:64, :] = jnp.concatenate(bands[:2], axis=1)
+    kp[64:96, :] = jnp.concatenate([bands[2][0:32], bands[2][32:64]], axis=1)
 
     mine = pl.ds(pl.multiple_of(48 * core, 16), 48)
     other = pl.ds(pl.multiple_of(48 * (1 - core), 16), 48)
@@ -308,15 +316,30 @@
     for j, target in enumerate((up, down, across)):
         gather.append(remote(quad.at[y], quad.at[y], b_send.at[j], b_recv.at[j], target))
     start(gather)
-    arrive(gather)
+
+    arrive(nears[4])
+    arrive(nears[5])
+    end = jnp.concatenate([heads(0, gn.at[0], HEAD[1::2]), heads(2, gn.at[1], HEAD[1::2])], axis=1)
+    late[aux] = jnp.concatenate([end[0:32], end[32:64]], axis=1)
+    for j, target in enumerate(peers):
+        gather.append(remote(late.at[aux], late.at[aux], b_send.at[3 + j], b_recv.at[3 + j], target))
+    start(gather[3:])
+    arrive(gather[:3])
     ob[mine, :] = (quad[0] + quad[1]) + (quad[2] + quad[3])
     share = remote(ob.at[mine, :], ob.at[mine, :], r_send.at[1], r_recv.at[1], sibling)
     share.start()
+    arrive(gather[3:])
+    total = late[0]
+    for j in range(1, 8):
+        total = total + late[j]
+    end = jnp.concatenate([total[:, 0:64], total[:, 64:128]], axis=0)
+    left, right = [end[:, 16 * j : 16 * j + 16] for j in range(2)], [end[:, 32 + 16 * j : 48 + 16 * j] for j in range(2)]
+    gap = jnp.zeros((64, 64), F32)
+    ends = jnp.concatenate([blank, left[0], blank, left[1], gap, blank, right[0], blank, right[1]], axis=1)
     share.wait_recv()
     pair.wait_send()
-    end = ob[64:96, :]
-    right = jnp.concatenate([end[:, 0:64], end[:, 64:128]], axis=0)
-    o_ref[...] = jnp.concatenate([ob[0:64, :], right], axis=1)
+    right = jnp.concatenate([ob[64:96, 0:64], ob[64:96, 64:128]], axis=0)
+    o_ref[...] = jnp.concatenate([ob[0:64, :], right], axis=1) + ends
     sent = coef + coef_on + sibs + gather + [share]
     for copies in owns + relays + nears:
         sent = sent + copies
@@ -353,8 +376,9 @@
             pltpu.VMEM((48, 128), F32),
             pltpu.VMEM((4, 48, 128), F32),
             pltpu.VMEM((96, 128), F32),
+            pltpu.VMEM((8, 32, 128), F32),
             dma((5,)), dma((n, 4)), dma((n, 4)), dma((n,)), dma((n,)), dma((4,)), dma((4,)),
-            dma((n, 2)), dma((n, 2)), dma((2,)), dma((2,)), dma((3,)), dma((3,)),
+            dma((n, 2)), dma((n, 2)), dma((2,)), dma((2,)), dma((10,)), dma((10,)),
         ],
         compiler_params=pltpu.CompilerParams(
             collective_id=0, has_side_effects=True, vmem_limit_bytes=62 * 1024 * 1024

time: 55.6 us -> 53.4 us (0.960)
  Pallas kernels: 53.9 us -> 51.7 us
    pallas_call x1, Pallas kernels: 53.9 us -> 51.7 us  [shards(): pl.pallas_call(functools.partial(kernel, n_orb), out_shape=jax.ShapeDtype...]
where the time goes in v3:
time: 53.4 us; the launch traced here: 53.2 us
  Pallas kernels  51.7 us (97%)
  local copies, waits for them, and re-layouts  1.47 us (3%)
    pallas_call x1, Pallas kernels, shards(): pl.pallas_call(functools.partial(kernel, n_orb), out_shape=jax.ShapeDtype...  51.7 us
    unnamed x1, local copies, waits for them, and re-layouts  1.47 us

profile of v3, /device:TPU:1, one launch (start us, length us, event | category | flops | bytes accessed | tf_op | source)
XLA Modules:
  0.0 53.2 jit_solution(7667498720735717386)
XLA Ops:
  0.0 51.7 %shard_map.46 = f32[64,192]{1,0:T(8,128)} custom-call(bf16[16,64,192]{2,1,0:T(8,128)(2,1)} %a_ref.1, bf16[64,1024]{1,0:T(8,128)(2,1)} %c_ref.1, bf16[128,128]{1,0:T(8,128)(2,1)} %metric_ref.1, s32[1,1,3]{2,1,0:T(1,128)} %screen_ref.1), custom_call_target="tpu_custom_call" | custom-call | tf_op jit(solution)/shard_map/pallas_call | solution.py:354
  51.7 1.5 %copy.6 = f32[64,192]{1,0:T(8,128)} copy(f32[64,192]{1,0:T(8,128)} %shard_map.46) | data formatting | bytes 98304

commit v4 on v3

--- a/solution.py
+++ b/solution.py
@@ -381,9 +381,9 @@
             dma((n, 2)), dma((n, 2)), dma((2,)), dma((2,)), dma((10,)), dma((10,)),
         ],
         compiler_params=pltpu.CompilerParams(
-            collective_id=0, has_side_effects=True, vmem_limit_bytes=62 * 1024 * 1024
+            collective_id=0, has_side_effects=True, vmem_limit_bytes=48 * 1024 * 1024
         ),
-    )(integrals, coefficients, metric, screening)
+    )(*[pltpu.with_memory_space_constraint(x, pltpu.HBM) for x in (integrals, coefficients, metric, screening)])
 
 
 def solution(mesh):

time: 53.4 us -> 51.9 us (0.972)
  local copies, waits for them, and re-layouts: 1.47 us -> 0.63 us
  Pallas kernels: 51.7 us -> 51.1 us
    unnamed x1, local copies, waits for them, and re-layouts: 1.47 us -> 0.63 us
    pallas_call x1, Pallas kernels: 51.7 us -> 51.1 us  [shards(): pl.pallas_call(functools.partial(kernel, n_orb), out_shape=jax.ShapeDtype...]
where the time goes in v4:
time: 51.9 us; the launch traced here: 51.7 us
  Pallas kernels  51.1 us (98%)
  local copies, waits for them, and re-layouts  0.63 us (1%)
    pallas_call x1, Pallas kernels, shards(): pl.pallas_call(functools.partial(kernel, n_orb), out_shape=jax.ShapeDtype...  51.1 us

profile of v4, /device:TPU:1, one launch (start us, length us, event | category | flops | bytes accessed | tf_op | source)
XLA Modules:
  0.0 51.7 jit_solution(12108959047704891936)
XLA Ops:
  0.0 51.1 %shard_map.46 = f32[64,192]{1,0:T(8,128)S(1)} custom-call(bf16[16,64,192]{2,1,0:T(8,128)(2,1)} %a_ref.1, bf16[64,1024]{1,0:T(8,128)(2,1)} %c_ref.1, bf16[128,128]{1,0:T(8,128)(2,1)} %metric_ref.1, s32[1,1,3]{2,1,0:T(1,128)} %screen_ref.1), custom_call_target="tpu_custom_call" | custom-call | tf_op jit(solution)/shard_map/pallas_call | solution.py:354
  51.1 0.6 %copy.6 = f32[64,192]{1,0:T(8,128)} copy(f32[64,192]{1,0:T(8,128)S(1)} %shard_map.46) | data formatting | bytes 98304

commit v5 on v4

--- a/solution.py
+++ b/solution.py
@@ -39,7 +39,7 @@
 def kernel(
     n_orb,
     a_ref, c_ref, metric_ref, screen_ref, o_ref,
-    av, m_ref, s_ref, cb, ag, mk, psend, precv, ghi, glo, gn, sp_hi, sp_lo, hh, ht, kp, kr, quad, ob, late,
+    av, m_ref, s_ref, cb, ag, mk, psend, precv, ghi, glo, gn, sp, hh, ht, kp, kr, quad, ob, late,
     load_sem, ag_send, ag_recv, sib_send, sib_recv, c_send, c_recv, g_send, g_recv, r_send, r_recv, b_send, b_recv,
 ):
     orb = lax.axis_index("orb")
@@ -166,12 +166,13 @@
             right = jnp.concatenate([cb[d], cb[d + 1], cb[d + 2], cb[d + 2]], axis=0)
             lanes = slice(256 * d, 256 * d + 256)
             zero = jnp.zeros((64, 256), BF16)
-            for part, dst in zip(split(nt(left, right)), (sp_hi, sp_lo)):
-                dst[0, 0:192, lanes] = part
-                dst[0, 192:256, lanes] = zero
-                dst[1, 0:128, lanes] = part[0:128]
-                dst[1, 128:192, lanes] = zero
-                dst[1, 192:256, lanes] = part[128:192]
+            high, low = split(nt(left, right))
+            for part, first in ((high, 0), (high, 256), (low, 512)):
+                sp[0, first : first + 192, lanes] = part
+                sp[0, first + 192 : first + 256, lanes] = zero
+                sp[1, first : first + 128, lanes] = part[0:128]
+                sp[1, first + 128 : first + 192, lanes] = zero
+                sp[1, first + 192 : first + 256, lanes] = part[128:192]
 
     def sib(c):
         t, n = CHUNKS[c]
@@ -194,9 +195,9 @@
     early = {}
 
     def premix(c):
-        t, n = CHUNKS[c]
-        panel = jnp.concatenate([ag[i, 0:768, :] for i in range(t, t + n)], axis=1)
-        early[c] = nn(mk[:, 0:768], panel)
+        panel = jnp.concatenate([ag[c, 0:768, :], ag[c + 1, 0:768, :]], axis=1)
+        out = nn(mk[:, 0:768], panel)
+        early[c], early[c + 1] = out[:, 0:128], out[:, 128:256]
 
     def mix(c):
         t, n = CHUNKS[c]
@@ -221,12 +222,10 @@
 
     def transform(group):
         par, h, t = group // 2, HEAD[group], TAIL[group % 2]
-        high = jnp.concatenate([ghi[h], ghi[t]], axis=1)
-        low = jnp.concatenate([glo[h], glo[t]], axis=1)
+        left = jnp.concatenate([ghi[h], ghi[t], glo[h], glo[t], ghi[h], ghi[t]], axis=1)
         for d in range(3):
             lanes = slice(256 * d, 256 * d + 256)
-            right = sp_hi[par, :, lanes]
-            out = nn(high, right) + nn(low, right) + nn(high, sp_lo[par, :, lanes])
+            out = nn(left, sp[par, :, lanes])
             for at, part in enumerate(split(out)):
                 row = slice(64 * at + 16 * group, 64 * at + 16 * group + 16)
                 hh[d, row, :] = fold(part[:, 0:128])
@@ -243,8 +242,8 @@
         out = nt(hh[d], panel_of(ref, tiles))
         return out[0:64] + out[64:128]
 
-    def tails(d, ref):
-        out = nt(ht[d], panel_of(ref, TAIL))
+    def tails(d, ref, which):
+        out = nt(ht[d], panel_of(ref, TAIL[which : which + 1]))
         return jnp.concatenate([out[0:64] + out[64:128], out[128:192] + out[192:256]], axis=1)
 
     def diagonal():
@@ -258,33 +257,30 @@
     arrive(owns[0])
     start(relays[0])
     start(owns[3])
-    premix(0)
     arrive(owns[1])
     start(relays[1])
     start(owns[4])
-    premix(1)
+    premix(0)
     arrive(coef)
     start(coef_on)
     arrive(owns[2])
     start(relays[2])
     start(owns[5])
-    premix(2)
     mix(0)
     arrive(owns[3])
     start(relays[3])
-    premix(3)
+    premix(2)
     mix(1)
     finish(0)
     arrive(owns[4])
     start(relays[4])
-    premix(4)
     mix(2)
     finish(1)
     gram()
     arrive(owns[5])
     start(relays[5])
     finish(2)
-    premix(5)
+    premix(4)
     mix(3)
     transform(0)
     mix(4)
@@ -296,18 +292,14 @@
     transform(1)
     transform(3)
 
-    bands = [None, diagonal(), None]
-    for c in range(4):
+    middle = diagonal()
+    for c in range(3):
         arrive(nears[c])
-    blank = jnp.zeros((64, 16), F32)
-    for d, ref in ((0, gn.at[0]), (2, gn.at[1])):
-        out = heads(d, ref, HEAD[0::2])
-        bands[d] = jnp.concatenate([out[:, 0:16], blank, out[:, 16:32], blank], axis=1) + tails(d, ref)
-    kp[0:64, :] = jnp.concatenate(bands[:2], axis=1)
-    kp[64:96, :] = jnp.concatenate([bands[2][0:32], bands[2][32:64]], axis=1)
-
-    mine = pl.ds(pl.multiple_of(48 * core, 16), 48)
-    other = pl.ds(pl.multiple_of(48 * (1 - core), 16), 48)
+    sides = [heads(d, gn.at[d // 2], HEAD[0::2]) + tails(d, gn.at[d // 2], 0) for d in (0, 2)]
+    kp[...] = jnp.concatenate([middle] + sides, axis=1)
+
+    mine = pl.ds(pl.multiple_of(32 * core, 16), 32)
+    other = pl.ds(pl.multiple_of(32 * (1 - core), 16), 32)
     pair = remote(kp.at[other, :], kr, r_send.at[0], r_recv.at[0], sibling)
     pair.start()
     pair.wait_recv()
@@ -317,13 +309,19 @@
         gather.append(remote(quad.at[y], quad.at[y], b_send.at[j], b_recv.at[j], target))
     start(gather)
 
+    arrive(nears[3])
+    ends = [tails(d, gn.at[d // 2], 1) for d in (0, 2)]
     arrive(nears[4])
     arrive(nears[5])
-    end = jnp.concatenate([heads(0, gn.at[0], HEAD[1::2]), heads(2, gn.at[1], HEAD[1::2])], axis=1)
+    ends = [ends[d // 2] + heads(d, gn.at[d // 2], HEAD[1::2]) for d in (0, 2)]
+    end = jnp.concatenate(ends, axis=1)
     late[aux] = jnp.concatenate([end[0:32], end[32:64]], axis=1)
     for j, target in enumerate(peers):
         gather.append(remote(late.at[aux], late.at[aux], b_send.at[3 + j], b_recv.at[3 + j], target))
     start(gather[3:])
+    for copies in owns + relays + nears + [coef, coef_on, sibs, gather[:3], [pair]]:
+        for copy in copies:
+            copy.wait_send()
     arrive(gather[:3])
     ob[mine, :] = (quad[0] + quad[1]) + (quad[2] + quad[3])
     share = remote(ob.at[mine, :], ob.at[mine, :], r_send.at[1], r_recv.at[1], sibling)
@@ -333,17 +331,13 @@
     for j in range(1, 8):
         total = total + late[j]
     end = jnp.concatenate([total[:, 0:64], total[:, 64:128]], axis=0)
-    left, right = [end[:, 16 * j : 16 * j + 16] for j in range(2)], [end[:, 32 + 16 * j : 48 + 16 * j] for j in range(2)]
-    gap = jnp.zeros((64, 64), F32)
-    ends = jnp.concatenate([blank, left[0], blank, left[1], gap, blank, right[0], blank, right[1]], axis=1)
     share.wait_recv()
-    pair.wait_send()
-    right = jnp.concatenate([ob[64:96, 0:64], ob[64:96, 64:128]], axis=0)
-    o_ref[...] = jnp.concatenate([ob[0:64, :], right], axis=1) + ends
-    sent = coef + coef_on + sibs + gather + [share]
-    for copies in owns + relays + nears:
-        sent = sent + copies
-    for copy in sent:
+    full = ob[...]
+    piece = lambda x, at: x[:, at : at + 16]
+    low = [piece(full, 64), piece(end, 0), piece(full, 80), piece(end, 16)]
+    high = [piece(full, 96), piece(end, 32), piece(full, 112), piece(end, 48)]
+    o_ref[...] = jnp.concatenate(low + [full[:, 0:64]] + high, axis=1)
+    for copy in gather[3:] + [share]:
         copy.wait_send()
 
 
@@ -368,14 +362,13 @@
             pltpu.VMEM((6, 256, 128), BF16),
             pltpu.VMEM((6, 256, 128), BF16),
             pltpu.VMEM((2, 6, 256, 128), BF16),
-            pltpu.VMEM((2, 256, 768), BF16),
-            pltpu.VMEM((2, 256, 768), BF16),
+            pltpu.VMEM((2, 768, 768), BF16),
             pltpu.VMEM((3, 128, 2048), BF16),
             pltpu.VMEM((3, 256, 2048), BF16),
-            pltpu.VMEM((96, 128), F32),
-            pltpu.VMEM((48, 128), F32),
-            pltpu.VMEM((4, 48, 128), F32),
-            pltpu.VMEM((96, 128), F32),
+            pltpu.VMEM((64, 128), F32),
+            pltpu.VMEM((32, 128), F32),
+            pltpu.VMEM((4, 32, 128), F32),
+            pltpu.VMEM((64, 128), F32),
             pltpu.VMEM((8, 32, 128), F32),
             dma((5,)), dma((n, 4)), dma((n, 4)), dma((n,)), dma((n,)), dma((4,)), dma((4,)),
             dma((n, 2)), dma((n, 2)), dma((2,)), dma((2,)), dma((10,)), dma((10,)),

time: 51.9 us -> 51.8 us (level)
  no operation moved by 1% of the time
where the time goes in v5:
time: 51.8 us; the launch traced here: 51.7 us
  Pallas kernels  51 us (98%)
  local copies, waits for them, and re-layouts  0.63 us (1%)
    pallas_call x1, Pallas kernels, shards(): pl.pallas_call(functools.partial(kernel, n_orb), out_shape=jax.ShapeDtype...  51 us

profile of v5, /device:TPU:1, one launch (start us, length us, event | category | flops | bytes accessed | tf_op | source)
XLA Modules:
  0.0 51.7 jit_solution(12306553221337576787)
XLA Ops:
  0.0 51.0 %shard_map.46 = f32[64,192]{1,0:T(8,128)S(1)} custom-call(bf16[16,64,192]{2,1,0:T(8,128)(2,1)} %a_ref.1, bf16[64,1024]{1,0:T(8,128)(2,1)} %c_ref.1, bf16[128,128]{1,0:T(8,128)(2,1)} %metric_ref.1, s32[1,1,3]{2,1,0:T(1,128)} %screen_ref.1), custom_call_target="tpu_custom_call" | custom-call | tf_op jit(solution)/shard_map/pallas_call | solution.py:348
  51.0 0.6 %copy.6 = f32[64,192]{1,0:T(8,128)} copy(f32[64,192]{1,0:T(8,128)S(1)} %shard_map.46) | data formatting | bytes 98304

commit v6 on v5

--- a/solution.py
+++ b/solution.py
@@ -226,7 +226,7 @@
         for d in range(3):
             lanes = slice(256 * d, 256 * d + 256)
             out = nn(left, sp[par, :, lanes])
-            for at, part in enumerate(split(out)):
+            for at, part in enumerate(split(out) if d == 1 else (out.astype(BF16),)):
                 row = slice(64 * at + 16 * group, 64 * at + 16 * group + 16)
                 hh[d, row, :] = fold(part[:, 0:128])
                 end = part[:, 128:256]
@@ -239,12 +239,11 @@
         return jnp.concatenate([fold(ref[t]) for t in tiles], axis=0)
 
     def heads(d, ref, tiles):
-        out = nt(hh[d], panel_of(ref, tiles))
-        return out[0:64] + out[64:128]
+        return nt(hh[d, 0:64, :], panel_of(ref, tiles))
 
     def tails(d, ref, which):
-        out = nt(ht[d], panel_of(ref, TAIL[which : which + 1]))
-        return jnp.concatenate([out[0:64] + out[64:128], out[128:192] + out[192:256]], axis=1)
+        panel = panel_of(ref, TAIL[which : which + 1])
+        return jnp.concatenate([nt(ht[d, 0:64, :], panel), nt(ht[d, 128:192, :], panel)], axis=1)
 
     def diagonal():
         out = nt(hh[1], jnp.concatenate([panel_of(ghi, HEAD), panel_of(glo, HEAD)], axis=0))

time: 51.8 us -> 51.6 us (level)
  no operation moved by 1% of the time
where the time goes in v6:
time: 51.6 us; the launch traced here: 51.4 us
  Pallas kernels  50.8 us (98%)
  local copies, waits for them, and re-layouts  0.63 us (1%)
    pallas_call x1, Pallas kernels, shards(): pl.pallas_call(functools.partial(kernel, n_orb), out_shape=jax.ShapeDtype...  50.8 us

profile of v6, /device:TPU:1, one launch (start us, length us, event | category | flops | bytes accessed | tf_op | source)
XLA Modules:
  0.0 51.4 jit_solution(13724526953846854986)
XLA Ops:
  0.0 50.8 %shard_map.46 = f32[64,192]{1,0:T(8,128)S(1)} custom-call(bf16[16,64,192]{2,1,0:T(8,128)(2,1)} %a_ref.1, bf16[64,1024]{1,0:T(8,128)(2,1)} %c_ref.1, bf16[128,128]{1,0:T(8,128)(2,1)} %metric_ref.1, s32[1,1,3]{2,1,0:T(1,128)} %screen_ref.1), custom_call_target="tpu_custom_call" | custom-call | tf_op jit(solution)/shard_map/pallas_call | solution.py:347
  50.8 0.6 %copy.6 = f32[64,192]{1,0:T(8,128)} copy(f32[64,192]{1,0:T(8,128)S(1)} %shard_map.46) | data formatting | bytes 98304
